TPU v7x, 32 devices: a whole 2x2x4 slice. The times are simulated.
32 devices in a mesh: req: 4 (over y, x), tm: 8 (over z, core).
Axes of the slice: x: 2, y: 2, z: 4, core: 2. Of those that a mesh axis runs over, the one named last changes fastest.
Arguments:
- latents: bfloat16 [32, 12288], P('req', 'tm'), may hold values from -6 to 6
- lengths: int32 [2], replicated, may hold values from 1 to 21, 32 in all
- w_in: bfloat16 [3, 3, 3, 16, 384], replicated, may hold values from -0.3125 to 0.3125
- b_in: float32 [384], replicated, may hold values from -3 to 3
- w_mid: bfloat16 [3, 3, 3, 384, 384], replicated, may hold values from -0.0625 to 0.0625
- b_mid: float32 [384], replicated, may hold values from -3 to 3
Outputs:
- decoded: bfloat16 [32, 64, 48, 384], P(('req', 'tm'))
Inputs may be any that keep to these rules, and one draw needn't show every extreme that they name: Request lengths in latent frames, in order along the frames, summing to 32; the longest has exactly 21.
All inputs are finite; a program needn't handle non-finite values.
Results may differ from a plain program's by a relative error of at most 0.0041.
Values may be sent and summed in bfloat16 or wider, within the bound.
A program may use at most 192 MiB of HBM per device.

v0:
```python
import functools

import jax
import jax.numpy as jnp
from jax import lax
from jax.experimental import pallas as pl
from jax.experimental.pallas import tpu as pltpu
from jax.sharding import PartitionSpec as P

F32 = jnp.float32
BF16 = jnp.bfloat16
MESH = pl.DeviceIdType.MESH
REACH = 4


def exchange_kernel(groups, members, lat_ref, out_ref, recv, send_sem, recv_sem, own_sem):
    r = lax.axis_index("req")
    me = lax.axis_index("tm")
    slots = REACH + 1
    has_next = r + 1 < groups
    has_prev = r > 0
    nxt = jnp.minimum(r + 1, groups - 1)
    prv = jnp.maximum(r - 1, 0)

    barrier = pltpu.get_barrier_semaphore()
    for t in range(members):

        @pl.when(me != t)
        def _():
            pl.semaphore_signal(barrier, inc=1, device_id=(r, jnp.int32(t)), device_id_type=MESH)

    @pl.when(has_prev & (me < REACH))
    def _():
        for t in range(members):
            pl.semaphore_signal(barrier, inc=1, device_id=(prv, jnp.int32(t)), device_id_type=MESH)

    @pl.when(has_next)
    def _():
        pl.semaphore_wait(barrier, members - 1 + REACH)

    @pl.when(jnp.logical_not(has_next))
    def _():
        pl.semaphore_wait(barrier, members - 1)

    def within(t, sender):
        count = min(t, REACH) + 1
        return lat_ref.at[pl.ds(t + 1 - count, count)], recv.at[sender, pl.ds(slots - count, count)]

    def across(t, sender):
        count = REACH - t
        return lat_ref.at[pl.ds(members - count, count)], recv.at[sender, pl.ds(0, count)]

    def near_copy(t):
        src, dst = within(t, me)
        return pltpu.make_async_remote_copy(
            src_ref=src,
            dst_ref=dst,
            send_sem=send_sem.at[t],
            recv_sem=recv_sem.at[0, me],
            device_id=(r, jnp.int32(t)),
            device_id_type=MESH,
        )

    def far_copy(t):
        src, dst = across(t, me)
        return pltpu.make_async_remote_copy(
            src_ref=src,
            dst_ref=dst,
            send_sem=send_sem.at[members + t],
            recv_sem=recv_sem.at[1, me],
            device_id=(nxt, jnp.int32(t)),
            device_id_type=MESH,
        )

    @pl.when(has_next)
    def _():
        for t in range(REACH):
            far_copy(t).start()

    for t in range(members):

        @pl.when(me != t)
        def _():
            near_copy(t).start()

        @pl.when(me == t)
        def _():
            src, dst = within(t, t)
            own = pltpu.make_async_copy(src, dst, own_sem)
            own.start()
            own.wait()

    for t in range(members):

        @pl.when(me == t)
        def _():
            for sender in range(members):
                if sender != t:
                    src, dst = within(t, sender)
                    pltpu.make_async_copy(src, dst, recv_sem.at[0, sender]).wait()
            if t < REACH:

                @pl.when(has_prev)
                def _():
                    for sender in range(members):
                        src, dst = across(t, sender)
                        pltpu.make_async_copy(src, dst, recv_sem.at[1, sender]).wait()

                @pl.when(jnp.logical_not(has_prev))
                def _():
                    for sender in range(members):
                        recv[sender, 0 : REACH - t] = jnp.zeros(
                            (REACH - t,) + recv.shape[2:], recv.dtype
                        )

    rows = recv.shape[2]
    for sender in range(members):
        for s in range(slots):
            out_ref[s, sender * rows : (sender + 1) * rows, :] = recv[sender, s].astype(F32)

    for t in range(members):

        @pl.when(me != t)
        def _():
            near_copy(t).wait_send()

    @pl.when(has_next)
    def _():
        for t in range(REACH):
            far_copy(t).wait_send()


def exchange(latents, groups, members, line):
    frames, feats = latents.shape
    rows = feats // line
    slots = REACH + 1
    pieces = latents.reshape(frames, rows, line)
    return pl.pallas_call(
        functools.partial(exchange_kernel, groups, members),
        out_shape=jax.ShapeDtypeStruct((slots, rows * members, line), F32),
        in_specs=[pl.BlockSpec(memory_space=pltpu.VMEM)],
        out_specs=pl.BlockSpec(memory_space=pltpu.VMEM),
        scratch_shapes=[
            pltpu.VMEM((members, slots, rows, line), BF16),
            pltpu.SemaphoreType.DMA((members + REACH,)),
            pltpu.SemaphoreType.DMA((2, members)),
            pltpu.SemaphoreType.DMA,
        ],
        compiler_params=pltpu.CompilerParams(collective_id=0, has_side_effects=True),
        name="exchange",
    )(pieces)


def decode_kernel(
    members, steps, ht, wt, c, ch,
    lengths_ref, x_ref, w_in_ref, b_in_ref, w_mid_ref, b_mid_ref, out_ref,
    raw, ws, wd, lh, ld, hb, sl, wide, raw_sem,
):
    step = pl.program_id(0)
    pos = ht * wt
    k_all = 3 * ch
    per = 128 // ht
    frame = lax.axis_index("req") * members + lax.axis_index("tm")

    def request_of(f):
        end = jnp.int32(0)
        count = jnp.int32(0)
        for r in range(lengths_ref.shape[0]):
            end = end + lengths_ref[r]
            count = count + (f >= end).astype(jnp.int32)
        return count

    def linked(earlier, f):
        return ((earlier >= 0) & (request_of(earlier) == request_of(f))) | (earlier == f)

    @pl.when(step == 0)
    def _prologue():
        for a in range(3):
            pltpu.make_async_copy(w_mid_ref.at[a], raw.at[a], raw_sem.at[a]).start()

        row_id = lax.broadcasted_iota(jnp.int32, (ht, wt * c), 0)
        quarter = lax.broadcasted_iota(jnp.int32, (c, 128), 1) // ht

        def spread(s, carry):
            x = jnp.where(frame - REACH + s >= 0, x_ref[s], 0.0)
            above = jnp.where(row_id == 0, 0.0, pltpu.roll(x, 1, 0))
            below = jnp.where(row_id == ht - 1, 0.0, pltpu.roll(x, ht - 1, 0))
            stacked = jnp.concatenate([above, x, below] + [jnp.zeros_like(x)] * (per - 3), axis=0)
            turned = stacked.T
            rolled = [turned] + [pltpu.roll(turned, ht * n, 1) for n in range(1, per)]
            zero = jnp.zeros((c, 128), F32)
            for di in range(3):
                for dj in range(3):
                    for jb in range(wt // per):
                        piece = zero
                        for jj in range(per):
                            j = jb * per + jj + dj - 1
                            if 0 <= j < wt:
                                part = rolled[(jj - di) % per][j * c : (j + 1) * c, :]
                                piece = jnp.where(quarter == jj, part, piece)
                        sl[s, pl.ds((di * 3 + dj) * c, c), pl.ds(jb * 128, 128)] = piece.astype(BF16)
            return carry

        lax.fori_loop(0, REACH + 1, spread, 0)

        edge = jnp.zeros((ht, 128), F32)
        for n in range(ch // 128):
            hb[n, pl.ds(0, ht, stride=wt), :] = edge
            hb[n, pl.ds(2 * pos + wt - 1, ht, stride=wt), :] = edge

        def first_layer(g, carry):
            f = frame - 2 + g
            acc = jnp.zeros((pos, ch), F32)
            for a in range(3):
                keep = linked(f - 2 + a, f)
                w = w_in_ref[a]
                w = jnp.where(keep, w, jnp.zeros_like(w))
                acc = acc + lax.dot_general(
                    sl[g + a], w, (((0,), (0,)), ((), ())), preferred_element_type=F32
                )
            v = acc + b_in_ref[...]
            h = (v / (1.0 + jnp.exp(-v))).astype(BF16).astype(F32)
            h = jnp.where(linked(f, frame), h, 0.0)
            for j in range(wt):
                for n in range(ch // 128):
                    part = h[j * ht : (j + 1) * ht, n * 128 : (n + 1) * 128]
                    hb[n, pl.ds(pos + j, ht, stride=wt), :] = part
                    if j < wt - 1:
                        hb[n, pl.ds(j + 1, ht, stride=wt), :] = part
                    if j > 0:
                        hb[n, pl.ds(2 * pos + j - 1, ht, stride=wt), :] = part
            z = jnp.zeros((wt, 128), F32)
            rest = jnp.zeros((ld.shape[0] - pos - wt, 128), F32)
            for v_at in range(3):
                for n in range(ch // 128):
                    lane = pl.ds(pl.multiple_of(v_at * k_all + g * ch + n * 128, 128), 128)
                    x = hb[n, pl.ds(v_at * pos, pos), :]
                    lh[:, lane] = x.astype(BF16)
                    d = jnp.concatenate([x, z, rest], 0) - jnp.concatenate([z, x, rest], 0)
                    ld[:, lane] = d.astype(BF16)
            return carry

        lax.fori_loop(0, 3, first_layer, 0)

        chunk = 32
        for a in range(3):
            pltpu.make_async_copy(w_mid_ref.at[a], raw.at[a], raw_sem.at[a]).wait()

            def combine(n, carry):
                at = pl.multiple_of(n * chunk, chunk)
                w = [[raw[a, p, q, pl.ds(at, chunk), :].astype(F32) for q in range(3)] for p in range(3)]
                s = [w[0][q] + w[1][q] + w[2][q] for q in range(3)]

                def columns(t):
                    return ((t[0], t[1] + t[2]), (t[0] + t[1], t[2]))

                s_c, u_c, l_c = columns(s), columns(w[0]), columns(w[2])
                for b in range(2):
                    for v in range(2):
                        dst = pl.ds(pl.multiple_of(v * k_all + a * ch + at, chunk), chunk)
                        ws[b, dst, :] = s_c[b][v].astype(BF16)
                        wd[b, dst, pl.ds(0, ch)] = u_c[b][v].astype(BF16)
                        wd[b, dst, pl.ds(ch, ch)] = l_c[b][v].astype(BF16)
                return carry

            lax.fori_loop(0, ch // chunk, combine, 0)

    lines = ht // steps
    m = lines * wt
    m_ext = m + 2 * 16
    row0 = pl.multiple_of(step * m, 16)
    for b in range(2):
        lane = pl.ds(b * k_all, 2 * k_all)
        ys = jnp.dot(lh[pl.ds(row0, m), lane], ws[b], preferred_element_type=F32) + b_mid_ref[...]
        yd = jnp.dot(ld[pl.ds(row0, m_ext), lane], wd[b], preferred_element_type=F32)
        y = (ys - yd[0:m, 0:ch], ys + yd[wt : wt + m, ch : 2 * ch])
        for i in range(lines):
            for a in range(2):
                for n in range(ch // 128):
                    wide[n, pl.ds((2 * i + a) * 2 * wt + b, wt, stride=2), :] = y[a][
                        i * wt : (i + 1) * wt, n * 128 : (n + 1) * 128
                    ]
    for i in range(2 * lines):
        for n in range(ch // 128):
            out_ref[i, :, n * 128 : (n + 1) * 128] = wide[n, pl.ds(i * 2 * wt, 2 * wt), :].astype(BF16)


def decode(x, lengths, w_in, b_in, w_mid, b_mid, members):
    slots, ht, line = x.shape
    c, ch = w_in.shape[-2:]
    wt = line // c
    pos = ht * wt
    steps = 2
    m = pos // steps
    vmem = pl.BlockSpec(memory_space=pltpu.VMEM)
    return pl.pallas_call(
        functools.partial(decode_kernel, members, steps, ht, wt, c, ch),
        grid=(steps,),
        out_shape=jax.ShapeDtypeStruct((2 * ht, 2 * wt, ch), BF16),
        in_specs=[
            pl.BlockSpec(memory_space=pltpu.SMEM),
            vmem, vmem, vmem,
            pl.BlockSpec(memory_space=pl.ANY),
            vmem,
        ],
        out_specs=pl.BlockSpec((2 * ht // steps, 2 * wt, ch), lambda i: (i, 0, 0)),
        scratch_shapes=[
            pltpu.VMEM(w_mid.shape, BF16),
            pltpu.VMEM((2, 6 * ch, ch), BF16),
            pltpu.VMEM((2, 6 * ch, 2 * ch), BF16),
            pltpu.VMEM((pos, 9 * ch), BF16),
            pltpu.VMEM((pos + 32, 9 * ch), BF16),
            pltpu.VMEM((ch // 128, 3 * pos, 128), F32),
            pltpu.VMEM((slots, 9 * c, pos), BF16),
            pltpu.VMEM((ch // 128, 4 * m, 128), F32),
            pltpu.SemaphoreType.DMA((3,)),
        ],
        compiler_params=pltpu.CompilerParams(vmem_limit_bytes=60 * 1024 * 1024),
        name="decode",
    )(lengths, x, w_in.reshape(3, 9 * c, ch), b_in.reshape(1, ch), w_mid, b_mid.reshape(1, ch))


def solution(mesh):
    groups, members = mesh.shape["req"], mesh.shape["tm"]

    def on_device(latents, lengths, w_in, b_in, w_mid, b_mid):
        c = w_in.shape[-2]
        line = 24 * c
        x = exchange(latents, groups, members, line)
        return decode(x, lengths, w_in, b_in, w_mid, b_mid, members)[None]

    in_specs = (P("req", "tm"), P(), P(), P(), P(), P())
    out_specs = P(("req", "tm"), None, None, None)
    return jax.shard_map(
        on_device, mesh=mesh, in_specs=in_specs, out_specs=out_specs, check_vma=False
    )
```

profile of v0, /device:TPU:0, one launch (start us, length us, event | category | flops | bytes accessed | tf_op | source)
XLA Modules:
  0.0 36.9 jit_solution(17776465015004511347)
XLA Ops:
  0.0 1.2 %reshape.14.b_in_ref = f32[1,384]{1,0:T(1,128)} reshape(f32[384]{0:T(512)} %param.9) | data formatting | bytes 3072 | tf_op jit(solution)/shard_map/reshape | solution.py:320
  1.2 1.3 %reshape.15.b_mid_ref = f32[1,384]{1,0:T(1,128)} reshape(f32[384]{0:T(512)} %param.11) | data formatting | bytes 3072 | tf_op jit(solution)/shard_map/reshape | solution.py:320
  2.5 1.4 %reshape.12.lat_ref = bf16[8,4,384]{2,1,0:T(4,128)(2,1)} reshape(bf16[8,1536]{1,0:T(8,128)(2,1)} %param.6) | data formatting | bytes 49152 | tf_op jit(solution)/shard_map/reshape | solution.py:137
  3.8 10.6 %exchange.1.x_ref = f32[5,32,384]{2,1,0:T(8,128)} custom-call(bf16[8,4,384]{2,1,0:T(4,128)(2,1)} %reshape.12.lat_ref), custom_call_target="tpu_custom_call" | custom-call | tf_op jit(solution)/shard_map/exchange/pallas_call | solution.py:138
  14.4 22.5 %decode.1 = bf16[64,48,384]{2,1,0:T(8,128)(2,1)} custom-call(s32[2]{0:T(128)} %lengths_ref.1, f32[5,32,384]{2,1,0:T(8,128)} %exchange.1.x_ref, bf16[3,144,384]{2,1,0:T(8,128)(2,1)} %bitcast.2, f32[1,384]{1,0:T(1,128)} %reshape.14.b_in_ref, bf16[3,3,3,384,384]{4,3,2,1,0:T(8,128)(2,1)} %w_mid_ref.1, f32[1,384]{1,0:T(1,128)} %reshape.15.b_mid_ref), custom_call_target="tpu_custom_call" | custom-call | tf_op jit(solution)/shard_map/decode/pallas_call | solution.py:296
where the time goes:
time: 37.2 us; the launch traced here: 36.9 us
  Pallas kernels  33 us (89%)
  local copies, waits for them, and re-layouts  3.84 us (10%)
    pallas_call x1, Pallas kernels, decode(): pl.pallas_call(functools.partial(decode_kernel, members, steps, ht, wt, c...  22.5 us
    pallas_call x1, Pallas kernels, exchange(): pl.pallas_call(functools.partial(exchange_kernel, groups, members), out_s...  10.6 us
    reshape x1, local copies, waits for them, and re-layouts, exchange(): pieces = latents.reshape(frames, rows, line)  1.36 us
    reshape x1, local copies, waits for them, and re-layouts, decode(): b_mid.reshape(1, ch)  1.25 us
    reshape x1, local copies, waits for them, and re-layouts, decode(): b_in.reshape(1, ch)  1.23 us

commit v1 on v0

--- a/solution.py
+++ b/solution.py
@@ -13,7 +13,11 @@
 REACH = 4
 
 
-def exchange_kernel(groups, members, lat_ref, out_ref, recv, send_sem, recv_sem, own_sem):
+def exchange_kernel(
+    groups, members, line,
+    lat_ref, w_mid_ref, out_ref, ws, wd,
+    stage, recv, raw, send_sem, recv_sem, own_sem, raw_sem,
+):
     r = lax.axis_index("req")
     me = lax.axis_index("tm")
     slots = REACH + 1
@@ -22,6 +26,11 @@
     nxt = jnp.minimum(r + 1, groups - 1)
     prv = jnp.maximum(r - 1, 0)
 
+    ch = w_mid_ref.shape[-1]
+    k_all = 3 * ch
+    for a in range(3):
+        pltpu.make_async_copy(w_mid_ref.at[a], raw.at[a], raw_sem.at[a]).start()
+
     barrier = pltpu.get_barrier_semaphore()
     for t in range(members):
 
@@ -34,6 +43,10 @@
         for t in range(members):
             pl.semaphore_signal(barrier, inc=1, device_id=(prv, jnp.int32(t)), device_id_type=MESH)
 
+    mine = lat_ref[...].astype(F32)
+    for u in range(lat_ref.shape[0]):
+        stage[u] = mine[u : u + 1, :].astype(BF16)
+
     @pl.when(has_next)
     def _():
         pl.semaphore_wait(barrier, members - 1 + REACH)
@@ -44,11 +57,11 @@
 
     def within(t, sender):
         count = min(t, REACH) + 1
-        return lat_ref.at[pl.ds(t + 1 - count, count)], recv.at[sender, pl.ds(slots - count, count)]
+        return stage.at[pl.ds(t + 1 - count, count)], recv.at[sender, pl.ds(slots - count, count)]
 
     def across(t, sender):
         count = REACH - t
-        return lat_ref.at[pl.ds(members - count, count)], recv.at[sender, pl.ds(0, count)]
+        return stage.at[pl.ds(members - count, count)], recv.at[sender, pl.ds(0, count)]
 
     def near_copy(t):
         src, dst = within(t, me)
@@ -90,6 +103,29 @@
             own.start()
             own.wait()
 
+    chunk = 32
+    for a in range(3):
+        pltpu.make_async_copy(w_mid_ref.at[a], raw.at[a], raw_sem.at[a]).wait()
+        def combine(n, carry):
+            at = pl.multiple_of(n * chunk, chunk)
+            w = [[raw[a, p, q, pl.ds(at, chunk), :].astype(F32) for q in range(3)] for p in range(3)]
+            s = [w[0][q] + w[1][q] + w[2][q] for q in range(3)]
+
+            def columns(t):
+                return ((t[0], t[1] + t[2]), (t[0] + t[1], t[2]))
+
+            s_c, u_c, l_c = columns(s), columns(w[0]), columns(w[2])
+            for b in range(2):
+                for v in range(2):
+                    dst = pl.ds(pl.multiple_of(v * k_all + a * ch + at, chunk), chunk)
+                    ws[b, dst, :] = s_c[b][v].astype(BF16)
+                    wd[b, dst, pl.ds(0, ch)] = u_c[b][v].astype(BF16)
+                    wd[b, dst, pl.ds(ch, ch)] = l_c[b][v].astype(BF16)
+            return carry
+
+        lax.fori_loop(0, ch // chunk, combine, 0)
+
+
     for t in range(members):
 
         @pl.when(me == t)
@@ -113,10 +149,12 @@
                             (REACH - t,) + recv.shape[2:], recv.dtype
                         )
 
-    rows = recv.shape[2]
+    rows = recv.shape[-1] // line
     for sender in range(members):
         for s in range(slots):
-            out_ref[s, sender * rows : (sender + 1) * rows, :] = recv[sender, s].astype(F32)
+            piece = recv[sender, s].astype(F32)
+            for n in range(rows):
+                out_ref[s, pl.ds(sender * rows + n, 1), :] = piece[:, n * line : (n + 1) * line]
 
     for t in range(members):
 
@@ -130,31 +168,44 @@
             far_copy(t).wait_send()
 
 
-def exchange(latents, groups, members, line):
+def exchange(latents, w_mid, groups, members, line):
     frames, feats = latents.shape
     rows = feats // line
     slots = REACH + 1
-    pieces = latents.reshape(frames, rows, line)
+    ch = w_mid.shape[-1]
+    vmem = pl.BlockSpec(memory_space=pltpu.VMEM)
+    hbm = pl.BlockSpec(memory_space=pl.ANY)
+    ws = (2, 6 * ch, ch)
+    wd = (2, 6 * ch, 2 * ch)
     return pl.pallas_call(
-        functools.partial(exchange_kernel, groups, members),
-        out_shape=jax.ShapeDtypeStruct((slots, rows * members, line), F32),
-        in_specs=[pl.BlockSpec(memory_space=pltpu.VMEM)],
-        out_specs=pl.BlockSpec(memory_space=pltpu.VMEM),
+        functools.partial(exchange_kernel, groups, members, line),
+        out_shape=(
+            jax.ShapeDtypeStruct((slots, rows * members, line), F32),
+            jax.ShapeDtypeStruct(ws, BF16),
+            jax.ShapeDtypeStruct(wd, BF16),
+        ),
+        in_specs=[vmem, hbm],
+        out_specs=(vmem, vmem, vmem),
         scratch_shapes=[
-            pltpu.VMEM((members, slots, rows, line), BF16),
+            pltpu.VMEM((frames, 1, feats), BF16),
+            pltpu.VMEM((members, slots, 1, feats), BF16),
+            pltpu.VMEM(w_mid.shape, BF16),
             pltpu.SemaphoreType.DMA((members + REACH,)),
             pltpu.SemaphoreType.DMA((2, members)),
             pltpu.SemaphoreType.DMA,
+            pltpu.SemaphoreType.DMA((3,)),
         ],
-        compiler_params=pltpu.CompilerParams(collective_id=0, has_side_effects=True),
+        compiler_params=pltpu.CompilerParams(
+            collective_id=0, has_side_effects=True, vmem_limit_bytes=46 * 1024 * 1024
+        ),
         name="exchange",
-    )(pieces)
+    )(latents, w_mid)
 
 
 def decode_kernel(
     members, steps, ht, wt, c, ch,
-    lengths_ref, x_ref, w_in_ref, b_in_ref, w_mid_ref, b_mid_ref, out_ref,
-    raw, ws, wd, lh, ld, hb, sl, wide, raw_sem,
+    lengths_ref, x_ref, w_in_ref, b_in_ref, ws, wd, b_mid_ref, out_ref,
+    lh, ld, hb, sl, wide,
 ):
     step = pl.program_id(0)
     pos = ht * wt
@@ -175,9 +226,6 @@
 
     @pl.when(step == 0)
     def _prologue():
-        for a in range(3):
-            pltpu.make_async_copy(w_mid_ref.at[a], raw.at[a], raw_sem.at[a]).start()
-
         row_id = lax.broadcasted_iota(jnp.int32, (ht, wt * c), 0)
         quarter = lax.broadcasted_iota(jnp.int32, (c, 128), 1) // ht
 
@@ -198,7 +246,8 @@
                             if 0 <= j < wt:
                                 part = rolled[(jj - di) % per][j * c : (j + 1) * c, :]
                                 piece = jnp.where(quarter == jj, part, piece)
-                        sl[s, pl.ds((di * 3 + dj) * c, c), pl.ds(jb * 128, 128)] = piece.astype(BF16)
+                        at = pl.multiple_of(s * 9 * c + (di * 3 + dj) * c, c)
+                        sl[pl.ds(at, c), pl.ds(jb * 128, 128)] = piece.astype(BF16)
             return carry
 
         lax.fori_loop(0, REACH + 1, spread, 0)
@@ -210,16 +259,18 @@
 
         def first_layer(g, carry):
             f = frame - 2 + g
-            acc = jnp.zeros((pos, ch), F32)
+            taps = []
             for a in range(3):
-                keep = linked(f - 2 + a, f)
                 w = w_in_ref[a]
-                w = jnp.where(keep, w, jnp.zeros_like(w))
-                acc = acc + lax.dot_general(
-                    sl[g + a], w, (((0,), (0,)), ((), ())), preferred_element_type=F32
-                )
-            v = acc + b_in_ref[...]
-            h = (v / (1.0 + jnp.exp(-v))).astype(BF16).astype(F32)
+                taps.append(jnp.where(linked(f - 2 + a, f), w, jnp.zeros_like(w)))
+            acc = lax.dot_general(
+                sl[pl.ds(pl.multiple_of(g * 9 * c, c), 27 * c), :],
+                jnp.concatenate(taps, 0),
+                (((0,), (0,)), ((), ())),
+                preferred_element_type=F32,
+            )
+            v = acc + b_in_ref[...][None, :]
+            h = (v * (0.5 + 0.5 * jnp.tanh(0.5 * v))).astype(BF16).astype(F32)
             h = jnp.where(linked(f, frame), h, 0.0)
             for j in range(wt):
                 for n in range(ch // 128):
@@ -242,28 +293,6 @@
 
         lax.fori_loop(0, 3, first_layer, 0)
 
-        chunk = 32
-        for a in range(3):
-            pltpu.make_async_copy(w_mid_ref.at[a], raw.at[a], raw_sem.at[a]).wait()
-
-            def combine(n, carry):
-                at = pl.multiple_of(n * chunk, chunk)
-                w = [[raw[a, p, q, pl.ds(at, chunk), :].astype(F32) for q in range(3)] for p in range(3)]
-                s = [w[0][q] + w[1][q] + w[2][q] for q in range(3)]
-
-                def columns(t):
-                    return ((t[0], t[1] + t[2]), (t[0] + t[1], t[2]))
-
-                s_c, u_c, l_c = columns(s), columns(w[0]), columns(w[2])
-                for b in range(2):
-                    for v in range(2):
-                        dst = pl.ds(pl.multiple_of(v * k_all + a * ch + at, chunk), chunk)
-                        ws[b, dst, :] = s_c[b][v].astype(BF16)
-                        wd[b, dst, pl.ds(0, ch)] = u_c[b][v].astype(BF16)
-                        wd[b, dst, pl.ds(ch, ch)] = l_c[b][v].astype(BF16)
-                return carry
-
-            lax.fori_loop(0, ch // chunk, combine, 0)
 
     lines = ht // steps
     m = lines * wt
@@ -271,7 +300,7 @@
     row0 = pl.multiple_of(step * m, 16)
     for b in range(2):
         lane = pl.ds(b * k_all, 2 * k_all)
-        ys = jnp.dot(lh[pl.ds(row0, m), lane], ws[b], preferred_element_type=F32) + b_mid_ref[...]
+        ys = jnp.dot(lh[pl.ds(row0, m), lane], ws[b], preferred_element_type=F32) + b_mid_ref[...][None, :]
         yd = jnp.dot(ld[pl.ds(row0, m_ext), lane], wd[b], preferred_element_type=F32)
         y = (ys - yd[0:m, 0:ch], ys + yd[wt : wt + m, ch : 2 * ch])
         for i in range(lines):
@@ -285,7 +314,7 @@
             out_ref[i, :, n * 128 : (n + 1) * 128] = wide[n, pl.ds(i * 2 * wt, 2 * wt), :].astype(BF16)
 
 
-def decode(x, lengths, w_in, b_in, w_mid, b_mid, members):
+def decode(x, lengths, w_in, b_in, ws, wd, b_mid, members):
     slots, ht, line = x.shape
     c, ch = w_in.shape[-2:]
     wt = line // c
@@ -299,25 +328,19 @@
         out_shape=jax.ShapeDtypeStruct((2 * ht, 2 * wt, ch), BF16),
         in_specs=[
             pl.BlockSpec(memory_space=pltpu.SMEM),
-            vmem, vmem, vmem,
-            pl.BlockSpec(memory_space=pl.ANY),
-            vmem,
+            vmem, vmem, vmem, vmem, vmem, vmem,
         ],
         out_specs=pl.BlockSpec((2 * ht // steps, 2 * wt, ch), lambda i: (i, 0, 0)),
         scratch_shapes=[
-            pltpu.VMEM(w_mid.shape, BF16),
-            pltpu.VMEM((2, 6 * ch, ch), BF16),
-            pltpu.VMEM((2, 6 * ch, 2 * ch), BF16),
             pltpu.VMEM((pos, 9 * ch), BF16),
             pltpu.VMEM((pos + 32, 9 * ch), BF16),
             pltpu.VMEM((ch // 128, 3 * pos, 128), F32),
-            pltpu.VMEM((slots, 9 * c, pos), BF16),
+            pltpu.VMEM((slots * 9 * c, pos), BF16),
             pltpu.VMEM((ch // 128, 4 * m, 128), F32),
-            pltpu.SemaphoreType.DMA((3,)),
         ],
-        compiler_params=pltpu.CompilerParams(vmem_limit_bytes=60 * 1024 * 1024),
+        compiler_params=pltpu.CompilerParams(vmem_limit_bytes=40 * 1024 * 1024),
         name="decode",
-    )(lengths, x, w_in.reshape(3, 9 * c, ch), b_in.reshape(1, ch), w_mid, b_mid.reshape(1, ch))
+    )(lengths, x, w_in.reshape(3, 9 * c, ch), b_in, ws, wd, b_mid)
 
 
 def solution(mesh):
@@ -326,8 +349,8 @@
     def on_device(latents, lengths, w_in, b_in, w_mid, b_mid):
         c = w_in.shape[-2]
         line = 24 * c
-        x = exchange(latents, groups, members, line)
-        return decode(x, lengths, w_in, b_in, w_mid, b_mid, members)[None]
+        x, ws, wd = exchange(latents, w_mid, groups, members, line)
+        return decode(x, lengths, w_in, b_in, ws, wd, b_mid, members)[None]
 
     in_specs = (P("req", "tm"), P(), P(), P(), P(), P())
     out_specs = P(("req", "tm"), None, None, None)

time: 37.2 us -> 37.5 us (level)
  Pallas kernels: 33 us -> 33.4 us
    pallas_call x1, Pallas kernels: 10.6 us -> 14.6 us  [exchange(): pl.pallas_call(functools.partial(exchange_kernel, groups, members, line),...]
    reshape x3 -> x0, local copies, waits for them, and re-layouts: 3.84 us -> none  [the longest x1 1.36 us: exchange(): pieces = latents.reshape(frames, rows, line)]
    unnamed x0 -> x12, local copies, waits for them, and re-layouts: none -> 3.8 us
    pallas_call x1, Pallas kernels: 22.5 us -> 18.9 us  [decode(): pl.pallas_call(functools.partial(decode_kernel, members, steps, ht, wt, c...]
where the time goes in v1:
time: 37.5 us; the launch traced here: 37.3 us
  Pallas kernels  33.4 us (89%)
  local copies, waits for them, and re-layouts  3.8 us (10%)
    pallas_call x1, Pallas kernels, decode(): pl.pallas_call(functools.partial(decode_kernel, members, steps, ht, wt, c...  18.9 us
    pallas_call x1, Pallas kernels, exchange(): pl.pallas_call(functools.partial(exchange_kernel, groups, members, line),...  14.6 us
    unnamed x12, local copies, waits for them, and re-layouts  3.8 us

profile of v1, /device:TPU:0, one launch (start us, length us, event | category | flops | bytes accessed | tf_op | source)
XLA Modules:
  0.0 37.3 jit_solution(17087134357191138073)
XLA Ops:
  0.0 0.0 copy-start.1
  0.0 0.0 copy-start.2
  0.0 0.8 %copy-done.2 = bf16[8,1536]{1,0:T(8,128)(2,1)S(1)} copy-done((bf16[8,1536]{1,0:T(8,128)(2,1)S(1)}, bf16[8,1536]{1,0:T(8,128)(2,1)}, u32[]{:S(2)}) %copy-start.2) | copy-done | bytes 24600
  0.8 0.0 copy-start.3
  0.8 0.0 copy-start.4
  0.8 0.0 copy-start.5
  0.8 14.6 %exchange.1 = (f32[5,32,384]{2,1,0:T(8,128)S(1)}, bf16[2,2304,384]{2,1,0:T(8,128)(2,1)S(1)}, bf16[2,2304,768]{2,1,0:T(8,128)(2,1)}) custom-call(bf16[8,1536]{1,0:T(8,128)(2,1)S(1)} %copy-done.2, bf16[3,3,3,384,384]{4,3,2,1,0:T(8,128)(2,1)} %w_mid_ref.1), custom_call_target="tpu_custom_call" | custom-call | tf_op jit(solution)/shard_map/exchange/pallas_call | solution.py:180
  15.4 0.0 copy-done.1
  15.4 0.0 copy-done.3
  15.4 0.0 copy-done.4
  15.4 0.0 copy-done.5
  15.4 0.0 copy-start
  15.4 3.0 %copy-done = bf16[2,2304,768]{2,1,0:T(8,128)(2,1)S(1)} copy-done((bf16[2,2304,768]{2,1,0:T(8,128)(2,1)S(1)}, bf16[2,2304,768]{2,1,0:T(8,128)(2,1)}, u32[]{:S(2)}) %copy-start) | copy-done | bytes 7077912
  18.4 18.9 %decode.1 = bf16[64,48,384]{2,1,0:T(8,128)(2,1)} custom-call(s32[2]{0:T(128)S(1)} %copy-done.5, f32[5,32,384]{2,1,0:T(8,128)S(1)} %get-tuple-element.8.x_ref, bf16[3,144,384]{2,1,0:T(8,128)(2,1)S(1)} %bitcast.2, f32[384]{0:T(512)S(1)} %copy-done.3, bf16[2,2304,384]{2,1,0:T(8,128)(2,1)S(1)} %get-tuple-element.9.ws, bf16[2,2304,768]{2,1,0:T(8,128)(2,1)S(1)} %copy-done, ...), custom_call_target="tpu_custom_call" | custom-call | tf_op jit(solution)/shard_map/decode/pallas_call | solution.py:325
Async XLA Ops:
  0.0 15.4 %copy-start.1 = (bf16[3,3,3,16,384]{4,3,2,1,0:T(8,128)(2,1)S(1)}, bf16[3,3,3,16,384]{4,3,2,1,0:T(8,128)(2,1)}, u32[]{:S(2)}) copy-start(bf16[3,3,3,16,384]{4,3,2,1,0:T(8,128)(2,1)} %param.8) | copy-start | bytes 995332
  0.0 0.8 %copy-start.2 = (bf16[8,1536]{1,0:T(8,128)(2,1)S(1)}, bf16[8,1536]{1,0:T(8,128)(2,1)}, u32[]{:S(2)}) copy-start(bf16[8,1536]{1,0:T(8,128)(2,1)} %lat_ref.1) | copy-start | bytes 73732
  0.8 14.6 %copy-start.3 = (f32[384]{0:T(512)S(1)}, f32[384]{0:T(512)}, u32[]{:S(2)}) copy-start(f32[384]{0:T(512)} %b_in_ref.1) | copy-start | bytes 4612
  0.8 14.6 %copy-start.4 = (f32[384]{0:T(512)S(1)}, f32[384]{0:T(512)}, u32[]{:S(2)}) copy-start(f32[384]{0:T(512)} %b_mid_ref.1) | copy-start | bytes 4612
  0.8 14.6 %copy-start.5 = (s32[2]{0:T(128)S(1)}, s32[2]{0:T(128)}, u32[]{:S(2)}) copy-start(s32[2]{0:T(128)} %lengths_ref.1) | copy-start | bytes 28
  15.4 3.0 %copy-start = (bf16[2,2304,768]{2,1,0:T(8,128)(2,1)S(1)}, bf16[2,2304,768]{2,1,0:T(8,128)(2,1)}, u32[]{:S(2)}) copy-start(bf16[2,2304,768]{2,1,0:T(8,128)(2,1)} %get-tuple-element.10.wd) | copy-start | bytes 21233668

commit v2 on v1

--- a/solution.py
+++ b/solution.py
@@ -101,39 +101,43 @@
             src, dst = within(t, t)
             own = pltpu.make_async_copy(src, dst, own_sem)
             own.start()
-            own.wait()
-
-    chunk = 32
+
+    chunk = 16
     for a in range(3):
         pltpu.make_async_copy(w_mid_ref.at[a], raw.at[a], raw_sem.at[a]).wait()
+
         def combine(n, carry):
             at = pl.multiple_of(n * chunk, chunk)
-            w = [[raw[a, p, q, pl.ds(at, chunk), :].astype(F32) for q in range(3)] for p in range(3)]
-            s = [w[0][q] + w[1][q] + w[2][q] for q in range(3)]
-
-            def columns(t):
-                return ((t[0], t[1] + t[2]), (t[0] + t[1], t[2]))
-
-            s_c, u_c, l_c = columns(s), columns(w[0]), columns(w[2])
-            for b in range(2):
-                for v in range(2):
-                    dst = pl.ds(pl.multiple_of(v * k_all + a * ch + at, chunk), chunk)
-                    ws[b, dst, :] = s_c[b][v].astype(BF16)
-                    wd[b, dst, pl.ds(0, ch)] = u_c[b][v].astype(BF16)
-                    wd[b, dst, pl.ds(ch, ch)] = l_c[b][v].astype(BF16)
+            for o in range(ch // 128):
+                lane = pl.ds(o * 128, 128)
+                w = [
+                    [raw[a, p, q, pl.ds(at, chunk), lane].astype(F32) for q in range(3)]
+                    for p in range(3)
+                ]
+                s = [w[0][q] + w[1][q] + w[2][q] for q in range(3)]
+
+                def columns(t):
+                    return ((t[0], t[1] + t[2]), (t[0] + t[1], t[2]))
+
+                s_c, u_c, l_c = columns(s), columns(w[0]), columns(w[2])
+                for b in range(2):
+                    for v in range(2):
+                        dst = pl.ds(pl.multiple_of(v * k_all + a * ch + at, chunk), chunk)
+                        ws[b, dst, lane] = s_c[b][v].astype(BF16)
+                        wd[b, dst, lane] = u_c[b][v].astype(BF16)
+                        wd[b, dst, pl.ds(ch + o * 128, 128)] = l_c[b][v].astype(BF16)
             return carry
 
         lax.fori_loop(0, ch // chunk, combine, 0)
 
-
     for t in range(members):
 
         @pl.when(me == t)
         def _():
             for sender in range(members):
-                if sender != t:
-                    src, dst = within(t, sender)
-                    pltpu.make_async_copy(src, dst, recv_sem.at[0, sender]).wait()
+                src, dst = within(t, sender)
+                sem = own_sem if sender == t else recv_sem.at[0, sender]
+                pltpu.make_async_copy(src, dst, sem).wait()
             if t < REACH:
 
                 @pl.when(has_prev)
@@ -196,7 +200,7 @@
             pltpu.SemaphoreType.DMA((3,)),
         ],
         compiler_params=pltpu.CompilerParams(
-            collective_id=0, has_side_effects=True, vmem_limit_bytes=46 * 1024 * 1024
+            collective_id=0, has_side_effects=True, vmem_limit_bytes=40 * 1024 * 1024
         ),
         name="exchange",
     )(latents, w_mid)
@@ -250,12 +254,10 @@
                         sl[pl.ds(at, c), pl.ds(jb * 128, 128)] = piece.astype(BF16)
             return carry
 
-        lax.fori_loop(0, REACH + 1, spread, 0)
-
-        edge = jnp.zeros((ht, 128), F32)
-        for n in range(ch // 128):
-            hb[n, pl.ds(0, ht, stride=wt), :] = edge
-            hb[n, pl.ds(2 * pos + wt - 1, ht, stride=wt), :] = edge
+        for s in range(REACH + 1):
+            spread(s, 0)
+
+        column = lax.broadcasted_iota(jnp.int32, (pos, 128), 0) % wt
 
         def first_layer(g, carry):
             f = frame - 2 + g
@@ -275,23 +277,21 @@
             for j in range(wt):
                 for n in range(ch // 128):
                     part = h[j * ht : (j + 1) * ht, n * 128 : (n + 1) * 128]
-                    hb[n, pl.ds(pos + j, ht, stride=wt), :] = part
-                    if j < wt - 1:
-                        hb[n, pl.ds(j + 1, ht, stride=wt), :] = part
-                    if j > 0:
-                        hb[n, pl.ds(2 * pos + j - 1, ht, stride=wt), :] = part
+                    hb[g, n, pl.ds(8 + j, ht, stride=wt), :] = part
             z = jnp.zeros((wt, 128), F32)
             rest = jnp.zeros((ld.shape[0] - pos - wt, 128), F32)
-            for v_at in range(3):
-                for n in range(ch // 128):
-                    lane = pl.ds(pl.multiple_of(v_at * k_all + g * ch + n * 128, 128), 128)
-                    x = hb[n, pl.ds(v_at * pos, pos), :]
+            for n in range(ch // 128):
+                left = jnp.where(column == 0, 0.0, hb[g, n, pl.ds(7, pos), :])
+                right = jnp.where(column == wt - 1, 0.0, hb[g, n, pl.ds(9, pos), :])
+                for v_at, x in enumerate((left, hb[g, n, pl.ds(8, pos), :], right)):
+                    lane = pl.ds(v_at * k_all + g * ch + n * 128, 128)
                     lh[:, lane] = x.astype(BF16)
                     d = jnp.concatenate([x, z, rest], 0) - jnp.concatenate([z, x, rest], 0)
                     ld[:, lane] = d.astype(BF16)
             return carry
 
-        lax.fori_loop(0, 3, first_layer, 0)
+        for g in range(3):
+            first_layer(g, 0)
 
 
     lines = ht // steps
@@ -334,7 +334,7 @@
         scratch_shapes=[
             pltpu.VMEM((pos, 9 * ch), BF16),
             pltpu.VMEM((pos + 32, 9 * ch), BF16),
-            pltpu.VMEM((ch // 128, 3 * pos, 128), F32),
+            pltpu.VMEM((3, ch // 128, pos + 16, 128), F32),
             pltpu.VMEM((slots * 9 * c, pos), BF16),
             pltpu.VMEM((ch // 128, 4 * m, 128), F32),
         ],

time: 37.5 us -> 30.1 us (0.80)
  Pallas kernels: 33.4 us -> 29.1 us
  local copies, waits for them, and re-layouts: 3.8 us -> 0.8 us
    unnamed x12 -> x10, local copies, waits for them, and re-layouts: 3.8 us -> 0.8 us
    pallas_call x1, Pallas kernels: 14.6 us -> 11.6 us  [exchange(): pl.pallas_call(functools.partial(exchange_kernel, groups, members, line),...]
    pallas_call x1, Pallas kernels: 18.9 us -> 17.5 us  [decode(): pl.pallas_call(functools.partial(decode_kernel, members, steps, ht, wt, c...]
where the time goes in v2:
time: 30.1 us; the launch traced here: 30 us
  Pallas kernels  29.1 us (97%)
  local copies, waits for them, and re-layouts  0.8 us (3%)
    pallas_call x1, Pallas kernels, decode(): pl.pallas_call(functools.partial(decode_kernel, members, steps, ht, wt, c...  17.5 us
    pallas_call x1, Pallas kernels, exchange(): pl.pallas_call(functools.partial(exchange_kernel, groups, members, line),...  11.6 us
    unnamed x10, local copies, waits for them, and re-layouts  0.8 us

profile of v2, /device:TPU:0, one launch (start us, length us, event | category | flops | bytes accessed | tf_op | source)
XLA Modules:
  0.0 30.0 jit_solution(3864814534290044596)
XLA Ops:
  0.0 0.0 copy-start
  0.0 0.0 copy-start.1
  0.0 0.8 %copy-done.1 = bf16[8,1536]{1,0:T(8,128)(2,1)S(1)} copy-done((bf16[8,1536]{1,0:T(8,128)(2,1)S(1)}, bf16[8,1536]{1,0:T(8,128)(2,1)}, u32[]{:S(2)}) %copy-start.1) | copy-done | bytes 24600
  0.8 0.0 copy-start.2
  0.8 0.0 copy-start.3
  0.8 0.0 copy-start.4
  0.8 11.6 %exchange.1 = (f32[5,32,384]{2,1,0:T(8,128)S(1)}, bf16[2,2304,384]{2,1,0:T(8,128)(2,1)S(1)}, bf16[2,2304,768]{2,1,0:T(8,128)(2,1)S(1)}) custom-call(bf16[8,1536]{1,0:T(8,128)(2,1)S(1)} %copy-done.1, bf16[3,3,3,384,384]{4,3,2,1,0:T(8,128)(2,1)} %w_mid_ref.1), custom_call_target="tpu_custom_call" | custom-call | tf_op jit(solution)/shard_map/exchange/pallas_call | solution.py:184
  12.5 0.0 copy-done
  12.5 0.0 copy-done.2
  12.5 0.0 copy-done.3
  12.5 0.0 copy-done.4
  12.5 17.5 %decode.1 = bf16[64,48,384]{2,1,0:T(8,128)(2,1)} custom-call(s32[2]{0:T(128)S(1)} %copy-done.4, f32[5,32,384]{2,1,0:T(8,128)S(1)} %get-tuple-element.8.x_ref, bf16[3,144,384]{2,1,0:T(8,128)(2,1)S(1)} %bitcast.2, f32[384]{0:T(512)S(1)} %copy-done.2, bf16[2,2304,384]{2,1,0:T(8,128)(2,1)S(1)} %get-tuple-element.9.ws, ...), custom_call_target="tpu_custom_call" | custom-call | tf_op jit(solution)/shard_map/decode/pallas_call | solution.py:325
Async XLA Ops:
  0.0 12.5 %copy-start = (bf16[3,3,3,16,384]{4,3,2,1,0:T(8,128)(2,1)S(1)}, bf16[3,3,3,16,384]{4,3,2,1,0:T(8,128)(2,1)}, u32[]{:S(2)}) copy-start(bf16[3,3,3,16,384]{4,3,2,1,0:T(8,128)(2,1)} %param.8) | copy-start | bytes 995332
  0.0 0.8 %copy-start.1 = (bf16[8,1536]{1,0:T(8,128)(2,1)S(1)}, bf16[8,1536]{1,0:T(8,128)(2,1)}, u32[]{:S(2)}) copy-start(bf16[8,1536]{1,0:T(8,128)(2,1)} %lat_ref.1) | copy-start | bytes 73732
  0.8 11.7 %copy-start.2 = (f32[384]{0:T(512)S(1)}, f32[384]{0:T(512)}, u32[]{:S(2)}) copy-start(f32[384]{0:T(512)} %b_in_ref.1) | copy-start | bytes 4612
  0.8 11.7 %copy-start.3 = (f32[384]{0:T(512)S(1)}, f32[384]{0:T(512)}, u32[]{:S(2)}) copy-start(f32[384]{0:T(512)} %b_mid_ref.1) | copy-start | bytes 4612
  0.8 11.7 %copy-start.4 = (s32[2]{0:T(128)S(1)}, s32[2]{0:T(128)}, u32[]{:S(2)}) copy-start(s32[2]{0:T(128)} %lengths_ref.1) | copy-start | bytes 28

commit v3 on v2

v3 whole, which is shorter than its diff:
```python
import functools

import jax
import jax.numpy as jnp
from jax import lax
from jax.experimental import pallas as pl
from jax.experimental.pallas import tpu as pltpu
from jax.sharding import PartitionSpec as P

F32 = jnp.float32
BF16 = jnp.bfloat16
MESH = pl.DeviceIdType.MESH
REACH = 4


def exchange_kernel(
    groups, members, line,
    lat_ref, w_mid_ref, out_ref, ws, wd,
    stage, recv, raw, send_sem, recv_sem, own_sem, raw_sem,
):
    r = lax.axis_index("req")
    me = lax.axis_index("tm")
    slots = REACH + 1
    has_next = r + 1 < groups
    has_prev = r > 0
    nxt = jnp.minimum(r + 1, groups - 1)
    prv = jnp.maximum(r - 1, 0)

    ch = w_mid_ref.shape[-1]
    for a in range(3):
        pltpu.make_async_copy(w_mid_ref.at[a], raw.at[a], raw_sem.at[a]).start()

    barrier = pltpu.get_barrier_semaphore()
    for t in range(members):

        @pl.when(me != t)
        def _():
            pl.semaphore_signal(barrier, inc=1, device_id=(r, jnp.int32(t)), device_id_type=MESH)

    @pl.when(has_prev & (me < REACH))
    def _():
        for t in range(members):
            pl.semaphore_signal(barrier, inc=1, device_id=(prv, jnp.int32(t)), device_id_type=MESH)

    chunk = 16

    def combine_tap(a):
        pltpu.make_async_copy(w_mid_ref.at[a], raw.at[a], raw_sem.at[a]).wait()

        def combine(n, carry):
            at = pl.multiple_of(n * chunk, chunk)
            for o in range(ch // 128):
                lane = pl.ds(o * 128, 128)
                w = [
                    [raw[a, p, q, pl.ds(at, chunk), lane].astype(F32) for q in range(3)]
                    for p in range(3)
                ]
                s = [w[0][q] + w[1][q] + w[2][q] for q in range(3)]

                def columns(t):
                    return ((t[0], t[1] + t[2]), (t[0] + t[1], t[2]))

                s_c, u_c, l_c = columns(s), columns(w[0]), columns(w[2])
                for b in range(2):
                    for v in range(2):
                        dst = pl.ds(pl.multiple_of((2 * a + v) * ch + at, chunk), chunk)
                        ws[b, dst, lane] = s_c[b][v].astype(BF16)
                        wd[b, dst, lane] = u_c[b][v].astype(BF16)
                        wd[b, dst, pl.ds(ch + o * 128, 128)] = l_c[b][v].astype(BF16)
            return carry

        lax.fori_loop(0, ch // chunk, combine, 0)

    mine = lat_ref[...].astype(F32)
    for u in range(lat_ref.shape[0]):
        stage[u] = mine[u : u + 1, :].astype(BF16)
    combine_tap(0)

    @pl.when(has_next)
    def _():
        pl.semaphore_wait(barrier, members - 1 + REACH)

    @pl.when(jnp.logical_not(has_next))
    def _():
        pl.semaphore_wait(barrier, members - 1)

    def within(t, sender):
        count = min(t, REACH) + 1
        return stage.at[pl.ds(t + 1 - count, count)], recv.at[sender, pl.ds(slots - count, count)]

    def across(t, sender):
        count = REACH - t
        return stage.at[pl.ds(members - count, count)], recv.at[sender, pl.ds(0, count)]

    def near_copy(t):
        src, dst = within(t, me)
        return pltpu.make_async_remote_copy(
            src_ref=src,
            dst_ref=dst,
            send_sem=send_sem.at[t],
            recv_sem=recv_sem.at[0, me],
            device_id=(r, jnp.int32(t)),
            device_id_type=MESH,
        )

    def far_copy(t):
        src, dst = across(t, me)
        return pltpu.make_async_remote_copy(
            src_ref=src,
            dst_ref=dst,
            send_sem=send_sem.at[members + t],
            recv_sem=recv_sem.at[1, me],
            device_id=(nxt, jnp.int32(t)),
            device_id_type=MESH,
        )

    @pl.when(has_next)
    def _():
        for t in range(REACH):
            far_copy(t).start()

    for t in range(members):

        @pl.when(me != t)
        def _():
            near_copy(t).start()

        @pl.when(me == t)
        def _():
            src, dst = within(t, t)
            own = pltpu.make_async_copy(src, dst, own_sem)
            own.start()

    combine_tap(1)
    combine_tap(2)

    for t in range(members):

        @pl.when(me == t)
        def _():
            for sender in range(members):
                src, dst = within(t, sender)
                sem = own_sem if sender == t else recv_sem.at[0, sender]
                pltpu.make_async_copy(src, dst, sem).wait()
            if t < REACH:

                @pl.when(has_prev)
                def _():
                    for sender in range(members):
                        src, dst = across(t, sender)
                        pltpu.make_async_copy(src, dst, recv_sem.at[1, sender]).wait()

                @pl.when(jnp.logical_not(has_prev))
                def _():
                    for sender in range(members):
                        recv[sender, 0 : REACH - t] = jnp.zeros(
                            (REACH - t,) + recv.shape[2:], recv.dtype
                        )

    rows = recv.shape[-1] // line
    for sender in range(members):
        for s in range(slots):
            piece = recv[sender, s].astype(F32)
            for n in range(rows):
                out_ref[s, pl.ds(sender * rows + n, 1), :] = piece[:, n * line : (n + 1) * line]

    for t in range(members):

        @pl.when(me != t)
        def _():
            near_copy(t).wait_send()

    @pl.when(has_next)
    def _():
        for t in range(REACH):
            far_copy(t).wait_send()


def exchange(latents, w_mid, groups, members, line):
    frames, feats = latents.shape
    rows = feats // line
    slots = REACH + 1
    ch = w_mid.shape[-1]
    vmem = pl.BlockSpec(memory_space=pltpu.VMEM)
    hbm = pl.BlockSpec(memory_space=pl.ANY)
    ws = (2, 6 * ch, ch)
    wd = (2, 6 * ch, 2 * ch)
    return pl.pallas_call(
        functools.partial(exchange_kernel, groups, members, line),
        out_shape=(
            jax.ShapeDtypeStruct((slots, rows * members, line), F32),
            jax.ShapeDtypeStruct(ws, BF16),
            jax.ShapeDtypeStruct(wd, BF16),
        ),
        in_specs=[vmem, hbm],
        out_specs=(vmem, vmem, vmem),
        scratch_shapes=[
            pltpu.VMEM((frames, 1, feats), BF16),
            pltpu.VMEM((members, slots, 1, feats), BF16),
            pltpu.VMEM(w_mid.shape, BF16),
            pltpu.SemaphoreType.DMA((members + REACH,)),
            pltpu.SemaphoreType.DMA((2, members)),
            pltpu.SemaphoreType.DMA,
            pltpu.SemaphoreType.DMA((3,)),
        ],
        compiler_params=pltpu.CompilerParams(
            collective_id=0, has_side_effects=True, vmem_limit_bytes=40 * 1024 * 1024
        ),
        name="exchange",
    )(latents, w_mid)


def decode_kernel(
    members, ht, wt, c, ch,
    lengths_ref, x_ref, w_in_ref, b_in_ref, ws, wd, b_mid_ref, out_ref,
    lh, ld, hb, sl, acc_s, acc_d, wide, done, out_sem,
):
    pos = ht * wt
    per = 128 // ht
    frame = lax.axis_index("req") * members + lax.axis_index("tm")

    def request_of(f):
        end = jnp.int32(0)
        count = jnp.int32(0)
        for r in range(lengths_ref.shape[0]):
            end = end + lengths_ref[r]
            count = count + (f >= end).astype(jnp.int32)
        return count

    def linked(earlier, f):
        return ((earlier >= 0) & (request_of(earlier) == request_of(f))) | (earlier == f)

    row_id = lax.broadcasted_iota(jnp.int32, (ht, wt * c), 0)
    quarter = lax.broadcasted_iota(jnp.int32, (c, 128), 1) // ht
    column = lax.broadcasted_iota(jnp.int32, (pos, 128), 0) % wt

    def spread(s):
        x = jnp.where(frame - REACH + s >= 0, x_ref[s], 0.0)
        above = jnp.where(row_id == 0, 0.0, pltpu.roll(x, 1, 0))
        below = jnp.where(row_id == ht - 1, 0.0, pltpu.roll(x, ht - 1, 0))
        stacked = jnp.concatenate([above, x, below] + [jnp.zeros_like(x)] * (per - 3), axis=0)
        turned = stacked.T
        rolled = [turned] + [pltpu.roll(turned, ht * n, 1) for n in range(1, per)]
        zero = jnp.zeros((c, 128), F32)
        for di in range(3):
            for dj in range(3):
                for jb in range(wt // per):
                    piece = zero
                    for jj in range(per):
                        j = jb * per + jj + dj - 1
                        if 0 <= j < wt:
                            part = rolled[(jj - di) % per][j * c : (j + 1) * c, :]
                            piece = jnp.where(quarter == jj, part, piece)
                    at = s * 9 * c + (di * 3 + dj) * c
                    sl[pl.ds(at, c), pl.ds(jb * 128, 128)] = piece.astype(BF16)

    parts = 2
    cols = wt // parts

    def first_layer(g, part):
        f = frame - 2 + g
        taps = []
        for a in range(3):
            w = w_in_ref[a]
            taps.append(jnp.where(linked(f - 2 + a, f), w, jnp.zeros_like(w)))
        acc = lax.dot_general(
            sl[pl.ds(g * 9 * c, 27 * c), pl.ds(part * cols * ht, cols * ht)],
            jnp.concatenate(taps, 0),
            (((0,), (0,)), ((), ())),
            preferred_element_type=F32,
        )
        v = acc + b_in_ref[...][None, :]
        h = (v * (0.5 + 0.5 * jnp.tanh(0.5 * v))).astype(BF16).astype(F32)
        h = jnp.where(linked(f, frame), h, 0.0)
        for j in range(cols):
            for n in range(ch // 128):
                hb[g, n, pl.ds(8 + part * cols + j, ht, stride=wt), :] = h[
                    j * ht : (j + 1) * ht, n * 128 : (n + 1) * 128
                ]

    def operands(g, n):
        z = jnp.zeros((wt, 128), F32)
        rest = jnp.zeros((ld.shape[1] - pos - wt, 128), F32)
        left = jnp.where(column == 0, 0.0, hb[g, n, pl.ds(7, pos), :])
        right = jnp.where(column == wt - 1, 0.0, hb[g, n, pl.ds(9, pos), :])
        for v_at, x in enumerate((left, hb[g, n, pl.ds(8, pos), :], right)):
            lane = pl.ds(v_at * ch + n * 128, 128)
            lh[g, :, lane] = x.astype(BF16)
            d = jnp.concatenate([x, z, rest], 0) - jnp.concatenate([z, x, rest], 0)
            ld[g, :, lane] = d.astype(BF16)

    def multiply(g, b, lhs, rhs, acc, at, width):
        depth = pl.ds(b * ch, 2 * ch)
        out = pl.ds(at, width)
        got = jnp.dot(
            lhs[g, :, depth], rhs[b, pl.ds(g * 2 * ch, 2 * ch), out], preferred_element_type=F32
        )
        if g == 0:
            acc[b, :, out] = got
        else:
            acc[b, :, out] += got

    def products(g, b):
        jobs = []
        for lhs, rhs, acc in ((lh, ws, acc_s), (ld, wd, acc_d)):
            for at in range(0, rhs.shape[-1], 256):
                width = min(256, rhs.shape[-1] - at)
                jobs.append(functools.partial(multiply, g, b, lhs, rhs, acc, at, width))
        return jobs

    def build(g):
        jobs = [functools.partial(first_layer, g, part) for part in range(parts)]
        return jobs + [functools.partial(operands, g, n) for n in range(ch // 128)]

    def place(b, n):
        lane = pl.ds(n * 128, 128)
        ys = acc_s[b, :, lane] + b_mid_ref[lane][None, :]
        y = (
            ys - acc_d[b, pl.ds(0, pos), lane],
            ys + acc_d[b, pl.ds(wt, pos), pl.ds(ch + n * 128, 128)],
        )
        for i in range(ht):
            for a in range(2):
                wide[n, pl.ds((2 * i + a) * 2 * wt + b, wt, stride=2), :] = y[a][
                    i * wt : (i + 1) * wt, :
                ]

    def mix(first, second):
        for k in range(max(len(first), len(second))):
            for jobs in (first, second):
                if k < len(jobs):
                    jobs[k]()

    for s in range(3):
        spread(s)
    for job in build(0):
        job()
    spread(3)
    mix(products(0, 0) + products(0, 1), build(1) + [functools.partial(spread, 4)])
    mix(products(1, 0) + products(1, 1), build(2))
    for job in products(2, 0):
        job()
    mix(products(2, 1), [functools.partial(place, 0, n) for n in range(ch // 128)])

    for n in range(ch // 128):
        place(1, n)
    cuts = 4
    rows = 2 * ht // cuts
    puts = []
    for cut in range(cuts):
        for i in range(cut * rows, (cut + 1) * rows):
            for n in range(ch // 128):
                done[i, :, n * 128 : (n + 1) * 128] = wide[n, pl.ds(i * 2 * wt, 2 * wt), :].astype(BF16)
        part = pl.ds(cut * rows, rows)
        puts.append(pltpu.make_async_copy(done.at[part], out_ref.at[part], out_sem.at[cut]))
        puts[-1].start()
    for put in puts:
        put.wait()


def decode(x, lengths, w_in, b_in, ws, wd, b_mid, members):
    slots, ht, line = x.shape
    c, ch = w_in.shape[-2:]
    wt = line // c
    pos = ht * wt
    vmem = pl.BlockSpec(memory_space=pltpu.VMEM)
    return pl.pallas_call(
        functools.partial(decode_kernel, members, ht, wt, c, ch),
        out_shape=jax.ShapeDtypeStruct((2 * ht, 2 * wt, ch), BF16),
        in_specs=[
            pl.BlockSpec(memory_space=pltpu.SMEM),
            vmem, vmem, vmem, vmem, vmem, vmem,
        ],
        out_specs=pl.BlockSpec(memory_space=pl.ANY),
        scratch_shapes=[
            pltpu.VMEM((3, pos, 3 * ch), BF16),
            pltpu.VMEM((3, pos + 32, 3 * ch), BF16),
            pltpu.VMEM((3, ch // 128, pos + 16, 128), F32),
            pltpu.VMEM((slots * 9 * c, pos), BF16),
            pltpu.VMEM((2, pos, ch), F32),
            pltpu.VMEM((2, pos + 32, 2 * ch), F32),
            pltpu.VMEM((ch // 128, 4 * pos, 128), F32),
            pltpu.VMEM((2 * ht, 2 * wt, ch), BF16),
            pltpu.SemaphoreType.DMA((4,)),
        ],
        compiler_params=pltpu.CompilerParams(vmem_limit_bytes=40 * 1024 * 1024),
        name="decode",
    )(lengths, x, w_in.reshape(3, 9 * c, ch), b_in, ws, wd, b_mid)


def solution(mesh):
    groups, members = mesh.shape["req"], mesh.shape["tm"]

    def on_device(latents, lengths, w_in, b_in, w_mid, b_mid):
        c = w_in.shape[-2]
        line = 24 * c
        x, ws, wd = exchange(latents, w_mid, groups, members, line)
        return decode(x, lengths, w_in, b_in, ws, wd, b_mid, members)[None]

    in_specs = (P("req", "tm"), P(), P(), P(), P(), P())
    out_specs = P(("req", "tm"), None, None, None)
    return jax.shard_map(
        on_device, mesh=mesh, in_specs=in_specs, out_specs=out_specs, check_vma=False
    )
```

time: 30.1 us -> 28.3 us (0.940)
  Pallas kernels: 29.1 us -> 27.3 us
    pallas_call x1, Pallas kernels: 17.5 us -> 14.9 us  [decode(): pl.pallas_call(functools.partial(decode_kernel, members, ht, wt, c, ch),...]
    pallas_call x1, Pallas kernels: 11.6 us -> 12.5 us  [exchange(): pl.pallas_call(functools.partial(exchange_kernel, groups, members, line),...]
where the time goes in v3:
time: 28.3 us; the launch traced here: 28.2 us
  Pallas kernels  27.3 us (96%)
  local copies, waits for them, and re-layouts  0.8 us (3%)
    pallas_call x1, Pallas kernels, decode(): pl.pallas_call(functools.partial(decode_kernel, members, ht, wt, c, ch),...  14.9 us
    pallas_call x1, Pallas kernels, exchange(): pl.pallas_call(functools.partial(exchange_kernel, groups, members, line),...  12.5 us
    unnamed x10, local copies, waits for them, and re-layouts  0.8 us

profile of v3, /device:TPU:0, one launch (start us, length us, event | category | flops | bytes accessed | tf_op | source)
XLA Modules:
  0.0 28.2 jit_solution(15213687084635131107)
XLA Ops:
  0.0 0.0 copy-start
  0.0 0.0 copy-start.1
  0.0 0.8 %copy-done.1 = bf16[8,1536]{1,0:T(8,128)(2,1)S(1)} copy-done((bf16[8,1536]{1,0:T(8,128)(2,1)S(1)}, bf16[8,1536]{1,0:T(8,128)(2,1)}, u32[]{:S(2)}) %copy-start.1) | copy-done | bytes 24600
  0.8 0.0 copy-start.2
  0.8 0.0 copy-start.3
  0.8 0.0 copy-start.4
  0.8 12.5 %exchange.1 = (f32[5,32,384]{2,1,0:T(8,128)S(1)}, bf16[2,2304,384]{2,1,0:T(8,128)(2,1)S(1)}, bf16[2,2304,768]{2,1,0:T(8,128)(2,1)S(1)}) custom-call(bf16[8,1536]{1,0:T(8,128)(2,1)S(1)} %copy-done.1, bf16[3,3,3,384,384]{4,3,2,1,0:T(8,128)(2,1)} %w_mid_ref.1), custom_call_target="tpu_custom_call" | custom-call | tf_op jit(solution)/shard_map/exchange/pallas_call | solution.py:188
  13.3 0.0 copy-done
  13.3 0.0 copy-done.2
  13.3 0.0 copy-done.3
  13.3 0.0 copy-done.4
  13.3 14.9 %decode.1 = bf16[64,48,384]{2,1,0:T(8,128)(2,1)} custom-call(s32[2]{0:T(128)S(1)} %copy-done.4, f32[5,32,384]{2,1,0:T(8,128)S(1)} %get-tuple-element.8.x_ref, bf16[3,144,384]{2,1,0:T(8,128)(2,1)S(1)} %bitcast.2, f32[384]{0:T(512)S(1)} %copy-done.2, bf16[2,2304,384]{2,1,0:T(8,128)(2,1)S(1)} %get-tuple-element.9.ws, ...), custom_call_target="tpu_custom_call" | custom-call | tf_op jit(solution)/shard_map/decode/pallas_call | solution.py:367
Async XLA Ops:
  0.0 13.3 %copy-start = (bf16[3,3,3,16,384]{4,3,2,1,0:T(8,128)(2,1)S(1)}, bf16[3,3,3,16,384]{4,3,2,1,0:T(8,128)(2,1)}, u32[]{:S(2)}) copy-start(bf16[3,3,3,16,384]{4,3,2,1,0:T(8,128)(2,1)} %param.8) | copy-start | bytes 995332
  0.0 0.8 %copy-start.1 = (bf16[8,1536]{1,0:T(8,128)(2,1)S(1)}, bf16[8,1536]{1,0:T(8,128)(2,1)}, u32[]{:S(2)}) copy-start(bf16[8,1536]{1,0:T(8,128)(2,1)} %lat_ref.1) | copy-start | bytes 73732
  0.8 12.5 %copy-start.2 = (f32[384]{0:T(512)S(1)}, f32[384]{0:T(512)}, u32[]{:S(2)}) copy-start(f32[384]{0:T(512)} %b_in_ref.1) | copy-start | bytes 4612
  0.8 12.5 %copy-start.3 = (f32[384]{0:T(512)S(1)}, f32[384]{0:T(512)}, u32[]{:S(2)}) copy-start(f32[384]{0:T(512)} %b_mid_ref.1) | copy-start | bytes 4612
  0.8 12.5 %copy-start.4 = (s32[2]{0:T(128)S(1)}, s32[2]{0:T(128)}, u32[]{:S(2)}) copy-start(s32[2]{0:T(128)} %lengths_ref.1) | copy-start | bytes 28

commit v4 on v3

--- a/solution.py
+++ b/solution.py
@@ -74,7 +74,6 @@
     mine = lat_ref[...].astype(F32)
     for u in range(lat_ref.shape[0]):
         stage[u] = mine[u : u + 1, :].astype(BF16)
-    combine_tap(0)
 
     @pl.when(has_next)
     def _():
@@ -131,8 +130,8 @@
             own = pltpu.make_async_copy(src, dst, own_sem)
             own.start()
 
-    combine_tap(1)
-    combine_tap(2)
+    for a in range(3):
+        combine_tap(a)
 
     for t in range(members):
 
@@ -289,71 +288,88 @@
             d = jnp.concatenate([x, z, rest], 0) - jnp.concatenate([z, x, rest], 0)
             ld[g, :, lane] = d.astype(BF16)
 
-    def multiply(g, b, lhs, rhs, acc, at, width):
+    def multiply(g, b, lhs, rhs, acc, at, width, rows):
         depth = pl.ds(b * ch, 2 * ch)
         out = pl.ds(at, width)
         got = jnp.dot(
-            lhs[g, :, depth], rhs[b, pl.ds(g * 2 * ch, 2 * ch), out], preferred_element_type=F32
+            lhs[g, rows, depth], rhs[b, pl.ds(g * 2 * ch, 2 * ch), out], preferred_element_type=F32
         )
         if g == 0:
-            acc[b, :, out] = got
+            acc[b, rows, out] = got
         else:
-            acc[b, :, out] += got
-
-    def products(g, b):
+            acc[b, rows, out] += got
+
+    half = pos // 2
+    every = (pl.ds(0, pos), pl.ds(0, pos + 32))
+    halves = (
+        (pl.ds(0, half), pl.ds(0, half + 32)),
+        (pl.ds(half, half), pl.ds(half + 32, half)),
+    )
+
+    def products(g, b, rows=every):
         jobs = []
-        for lhs, rhs, acc in ((lh, ws, acc_s), (ld, wd, acc_d)):
+        for lhs, rhs, acc, own in ((lh, ws, acc_s, rows[0]), (ld, wd, acc_d, rows[1])):
             for at in range(0, rhs.shape[-1], 256):
                 width = min(256, rhs.shape[-1] - at)
-                jobs.append(functools.partial(multiply, g, b, lhs, rhs, acc, at, width))
+                jobs.append(functools.partial(multiply, g, b, lhs, rhs, acc, at, width, own))
         return jobs
 
     def build(g):
         jobs = [functools.partial(first_layer, g, part) for part in range(parts)]
         return jobs + [functools.partial(operands, g, n) for n in range(ch // 128)]
 
-    def place(b, n):
+    def place(b, n, at):
         lane = pl.ds(n * 128, 128)
-        ys = acc_s[b, :, lane] + b_mid_ref[lane][None, :]
+        top = at * half
+        ys = acc_s[b, pl.ds(top, half), lane] + b_mid_ref[lane][None, :]
         y = (
-            ys - acc_d[b, pl.ds(0, pos), lane],
-            ys + acc_d[b, pl.ds(wt, pos), pl.ds(ch + n * 128, 128)],
+            ys - acc_d[b, pl.ds(top, half), lane],
+            ys + acc_d[b, pl.ds(top + wt, half), pl.ds(ch + n * 128, 128)],
         )
-        for i in range(ht):
+        for i in range(ht // 2):
             for a in range(2):
-                wide[n, pl.ds((2 * i + a) * 2 * wt + b, wt, stride=2), :] = y[a][
-                    i * wt : (i + 1) * wt, :
-                ]
-
-    def mix(first, second):
-        for k in range(max(len(first), len(second))):
-            for jobs in (first, second):
-                if k < len(jobs):
-                    jobs[k]()
-
-    for s in range(3):
-        spread(s)
-    for job in build(0):
-        job()
-    spread(3)
-    mix(products(0, 0) + products(0, 1), build(1) + [functools.partial(spread, 4)])
-    mix(products(1, 0) + products(1, 1), build(2))
-    for job in products(2, 0):
-        job()
-    mix(products(2, 1), [functools.partial(place, 0, n) for n in range(ch // 128)])
-
-    for n in range(ch // 128):
-        place(1, n)
-    cuts = 4
-    rows = 2 * ht // cuts
+                row = at * ht + 2 * i + a
+                wide[n, pl.ds(row * 2 * wt + b, wt, stride=2), :] = y[a][i * wt : (i + 1) * wt, :]
+
     puts = []
-    for cut in range(cuts):
+
+    def finish(cut):
+        rows = 2 * ht // 4
         for i in range(cut * rows, (cut + 1) * rows):
             for n in range(ch // 128):
                 done[i, :, n * 128 : (n + 1) * 128] = wide[n, pl.ds(i * 2 * wt, 2 * wt), :].astype(BF16)
         part = pl.ds(cut * rows, rows)
         puts.append(pltpu.make_async_copy(done.at[part], out_ref.at[part], out_sem.at[cut]))
         puts[-1].start()
+
+    def placing(at):
+        return [functools.partial(place, b, n, at) for b in range(2) for n in range(ch // 128)]
+
+    def mix(first, second):
+        for k in range(max(len(first), len(second))):
+            for jobs in (first, second):
+                if k < len(jobs):
+                    jobs[k]()
+
+    for s in range(3):
+        spread(s)
+    for job in build(0):
+        job()
+    mix(
+        products(0, 0) + products(0, 1),
+        [functools.partial(spread, 3)] + build(1) + [functools.partial(spread, 4)],
+    )
+    mix(products(1, 0) + products(1, 1), build(2))
+    for job in products(2, 0, halves[0]) + products(2, 1, halves[0]):
+        job()
+    mix(
+        products(2, 0, halves[1]) + products(2, 1, halves[1]),
+        placing(0) + [functools.partial(finish, cut) for cut in range(2)],
+    )
+    for job in placing(1):
+        job()
+    for cut in range(2, 4):
+        finish(cut)
     for put in puts:
         put.wait()
 

time: 28.3 us -> 27.4 us (0.968)
  Pallas kernels: 27.3 us -> 26.4 us
    pallas_call x1, Pallas kernels: 12.5 us -> 11.6 us  [exchange(): pl.pallas_call(functools.partial(exchange_kernel, groups, members, line),...]
where the time goes in v4:
time: 27.4 us; the launch traced here: 27.3 us
  Pallas kernels  26.4 us (96%)
  local copies, waits for them, and re-layouts  0.8 us (3%)
    pallas_call x1, Pallas kernels, decode(): pl.pallas_call(functools.partial(decode_kernel, members, ht, wt, c, ch),...  14.8 us
    pallas_call x1, Pallas kernels, exchange(): pl.pallas_call(functools.partial(exchange_kernel, groups, members, line),...  11.6 us
    unnamed x10, local copies, waits for them, and re-layouts  0.8 us

profile of v4, /device:TPU:0, one launch (start us, length us, event | category | flops | bytes accessed | tf_op | source)
XLA Modules:
  0.0 27.3 jit_solution(11130878029474647707)
XLA Ops:
  0.0 0.0 copy-start
  0.0 0.0 copy-start.1
  0.0 0.8 %copy-done.1 = bf16[8,1536]{1,0:T(8,128)(2,1)S(1)} copy-done((bf16[8,1536]{1,0:T(8,128)(2,1)S(1)}, bf16[8,1536]{1,0:T(8,128)(2,1)}, u32[]{:S(2)}) %copy-start.1) | copy-done | bytes 24600
  0.8 0.0 copy-start.2
  0.8 0.0 copy-start.3
  0.8 0.0 copy-start.4
  0.8 11.6 %exchange.1 = (f32[5,32,384]{2,1,0:T(8,128)S(1)}, bf16[2,2304,384]{2,1,0:T(8,128)(2,1)S(1)}, bf16[2,2304,768]{2,1,0:T(8,128)(2,1)S(1)}) custom-call(bf16[8,1536]{1,0:T(8,128)(2,1)S(1)} %copy-done.1, bf16[3,3,3,384,384]{4,3,2,1,0:T(8,128)(2,1)} %w_mid_ref.1), custom_call_target="tpu_custom_call" | custom-call | tf_op jit(solution)/shard_map/exchange/pallas_call | solution.py:187
  12.5 0.0 copy-done
  12.5 0.0 copy-done.2
  12.5 0.0 copy-done.3
  12.5 0.0 copy-done.4
  12.5 14.8 %decode.1 = bf16[64,48,384]{2,1,0:T(8,128)(2,1)} custom-call(s32[2]{0:T(128)S(1)} %copy-done.4, f32[5,32,384]{2,1,0:T(8,128)S(1)} %get-tuple-element.8.x_ref, bf16[3,144,384]{2,1,0:T(8,128)(2,1)S(1)} %bitcast.2, f32[384]{0:T(512)S(1)} %copy-done.2, bf16[2,2304,384]{2,1,0:T(8,128)(2,1)S(1)} %get-tuple-element.9.ws, ...), custom_call_target="tpu_custom_call" | custom-call | tf_op jit(solution)/shard_map/decode/pallas_call | solution.py:383
Async XLA Ops:
  0.0 12.5 %copy-start = (bf16[3,3,3,16,384]{4,3,2,1,0:T(8,128)(2,1)S(1)}, bf16[3,3,3,16,384]{4,3,2,1,0:T(8,128)(2,1)}, u32[]{:S(2)}) copy-start(bf16[3,3,3,16,384]{4,3,2,1,0:T(8,128)(2,1)} %param.8) | copy-start | bytes 995332
  0.0 0.8 %copy-start.1 = (bf16[8,1536]{1,0:T(8,128)(2,1)S(1)}, bf16[8,1536]{1,0:T(8,128)(2,1)}, u32[]{:S(2)}) copy-start(bf16[8,1536]{1,0:T(8,128)(2,1)} %lat_ref.1) | copy-start | bytes 73732
  0.8 11.7 %copy-start.2 = (f32[384]{0:T(512)S(1)}, f32[384]{0:T(512)}, u32[]{:S(2)}) copy-start(f32[384]{0:T(512)} %b_in_ref.1) | copy-start | bytes 4612
  0.8 11.7 %copy-start.3 = (f32[384]{0:T(512)S(1)}, f32[384]{0:T(512)}, u32[]{:S(2)}) copy-start(f32[384]{0:T(512)} %b_mid_ref.1) | copy-start | bytes 4612
  0.8 11.7 %copy-start.4 = (s32[2]{0:T(128)S(1)}, s32[2]{0:T(128)}, u32[]{:S(2)}) copy-start(s32[2]{0:T(128)} %lengths_ref.1) | copy-start | bytes 28

commit v5 on v4

--- a/solution.py
+++ b/solution.py
@@ -309,9 +309,7 @@
     def products(g, b, rows=every):
         jobs = []
         for lhs, rhs, acc, own in ((lh, ws, acc_s, rows[0]), (ld, wd, acc_d, rows[1])):
-            for at in range(0, rhs.shape[-1], 256):
-                width = min(256, rhs.shape[-1] - at)
-                jobs.append(functools.partial(multiply, g, b, lhs, rhs, acc, at, width, own))
+            jobs.append(functools.partial(multiply, g, b, lhs, rhs, acc, 0, rhs.shape[-1], own))
         return jobs
 
     def build(g):

time: 27.4 us -> 27.4 us (level)
  no operation moved by 1% of the time
where the time goes in v5:
time: 27.4 us; the launch traced here: 27.3 us
  Pallas kernels  26.4 us (96%)
  local copies, waits for them, and re-layouts  0.8 us (3%)
    pallas_call x1, Pallas kernels, decode(): pl.pallas_call(functools.partial(decode_kernel, members, ht, wt, c, ch),...  14.8 us
    pallas_call x1, Pallas kernels, exchange(): pl.pallas_call(functools.partial(exchange_kernel, groups, members, line),...  11.6 us
    unnamed x10, local copies, waits for them, and re-layouts  0.8 us

profile of v5, /device:TPU:0, one launch (start us, length us, event | category | flops | bytes accessed | tf_op | source)
XLA Modules:
  0.0 27.3 jit_solution(16568904247414464778)
XLA Ops:
  0.0 0.0 copy-start
  0.0 0.0 copy-start.1
  0.0 0.8 %copy-done.1 = bf16[8,1536]{1,0:T(8,128)(2,1)S(1)} copy-done((bf16[8,1536]{1,0:T(8,128)(2,1)S(1)}, bf16[8,1536]{1,0:T(8,128)(2,1)}, u32[]{:S(2)}) %copy-start.1) | copy-done | bytes 24600
  0.8 0.0 copy-start.2
  0.8 0.0 copy-start.3
  0.8 0.0 copy-start.4
  0.8 11.6 %exchange.1 = (f32[5,32,384]{2,1,0:T(8,128)S(1)}, bf16[2,2304,384]{2,1,0:T(8,128)(2,1)S(1)}, bf16[2,2304,768]{2,1,0:T(8,128)(2,1)S(1)}) custom-call(bf16[8,1536]{1,0:T(8,128)(2,1)S(1)} %copy-done.1, bf16[3,3,3,384,384]{4,3,2,1,0:T(8,128)(2,1)} %w_mid_ref.1), custom_call_target="tpu_custom_call" | custom-call | tf_op jit(solution)/shard_map/exchange/pallas_call | solution.py:187
  12.5 0.0 copy-done
  12.5 0.0 copy-done.2
  12.5 0.0 copy-done.3
  12.5 0.0 copy-done.4
  12.5 14.8 %decode.1 = bf16[64,48,384]{2,1,0:T(8,128)(2,1)} custom-call(s32[2]{0:T(128)S(1)} %copy-done.4, f32[5,32,384]{2,1,0:T(8,128)S(1)} %get-tuple-element.8.x_ref, bf16[3,144,384]{2,1,0:T(8,128)(2,1)S(1)} %bitcast.2, f32[384]{0:T(512)S(1)} %copy-done.2, bf16[2,2304,384]{2,1,0:T(8,128)(2,1)S(1)} %get-tuple-element.9.ws, ...), custom_call_target="tpu_custom_call" | custom-call | tf_op jit(solution)/shard_map/decode/pallas_call | solution.py:381
Async XLA Ops:
  0.0 12.5 %copy-start = (bf16[3,3,3,16,384]{4,3,2,1,0:T(8,128)(2,1)S(1)}, bf16[3,3,3,16,384]{4,3,2,1,0:T(8,128)(2,1)}, u32[]{:S(2)}) copy-start(bf16[3,3,3,16,384]{4,3,2,1,0:T(8,128)(2,1)} %param.8) | copy-start | bytes 995332
  0.0 0.8 %copy-start.1 = (bf16[8,1536]{1,0:T(8,128)(2,1)S(1)}, bf16[8,1536]{1,0:T(8,128)(2,1)}, u32[]{:S(2)}) copy-start(bf16[8,1536]{1,0:T(8,128)(2,1)} %lat_ref.1) | copy-start | bytes 73732
  0.8 11.7 %copy-start.2 = (f32[384]{0:T(512)S(1)}, f32[384]{0:T(512)}, u32[]{:S(2)}) copy-start(f32[384]{0:T(512)} %b_in_ref.1) | copy-start | bytes 4612
  0.8 11.7 %copy-start.3 = (f32[384]{0:T(512)S(1)}, f32[384]{0:T(512)}, u32[]{:S(2)}) copy-start(f32[384]{0:T(512)} %b_mid_ref.1) | copy-start | bytes 4612
  0.8 11.7 %copy-start.4 = (s32[2]{0:T(128)S(1)}, s32[2]{0:T(128)}, u32[]{:S(2)}) copy-start(s32[2]{0:T(128)} %lengths_ref.1) | copy-start | bytes 28
